TPU v7x, 128 devices: a whole 4x4x4 slice. The times are simulated.
128 devices in a mesh: depth: 8 (over y_lo, z), rows: 2 (over core), cols: 8 (over x, y_hi).
Axes of the slice: x: 4, y: 4 (y_hi: 2, y_lo: 2; y = y_hi * 2 + y_lo), z: 4, core: 2. Of those that a mesh axis runs over, the one named last changes fastest.
Arguments:
- lower_panels: bfloat16 [16, 8, 768, 1024], P('depth', None, None, ('rows', 'cols')), may hold values from -0.23925781 to 0.23925781
- upper_panels: bfloat16 [16, 1024, 6144], P('depth', 'rows', 'cols'), may hold values from -0.23925781 to 0.23925781
- given_inverse: bfloat16 [16, 1024, 1024], P('depth', 'rows'), may hold values from -0.05625 to 2, as said below
- structure: int32 [16, 48], P('depth'), may hold values 0 or 1
- ancestor_entries: float32 [6144, 6144], P(('depth', 'rows'), 'cols'), may hold values from -0.6 to 19.2, as said below
Outputs:
- column_factor: float32 [6144, 512], P(('depth', 'rows'))
- trailing: float32 [6144, 6144], P(('depth', 'rows'), 'cols')
Inputs may be any that keep to these rules, and one draw needn't show every extreme that they name: `given_inverse`: off-diagonal entries are small against the diagonal. `ancestor_entries`: diagonal entries lie between 12.8 and 19.2.
All inputs are finite; a program needn't handle non-finite values. No bound on the sum of `structure` on one device may be relied on, other than what follows from the above.
Results may differ from a plain program's by a relative error of at most 0.0003.
Values may be sent and summed in bfloat16 or wider, within the bound.
A program may use at most 128 MiB of HBM per device.

v0:
```python
import jax
import jax.numpy as jnp
from jax import lax
from jax.sharding import PartitionSpec as P

PW = 512
NEWTON = 2


def from_root(array, axis, root):
    mine = lax.axis_index(axis) == root
    return lax.psum(jnp.where(mine, array, jnp.zeros_like(array)), axis)


def local(lower_panels, upper_panels, given_inverse, structure, ancestor_entries):
    highest = lax.Precision.HIGHEST
    subtree_count = lower_panels.shape[0]
    depth_count = lax.axis_size("depth")
    rows_count = lax.axis_size("rows")
    block_rows = lower_panels.shape[2]
    local_cols = upper_panels.shape[2]
    row_share = block_rows // rows_count
    block_count = structure.shape[1]
    block_size = depth_count * block_rows // block_count
    kept_blocks = (structure != 0).astype(jnp.bfloat16)
    lower_masked = (
        lower_panels.reshape(subtree_count, block_count, block_size, lower_panels.shape[3])
        * kept_blocks[:, :, None, None]
    ).reshape(lower_panels.shape)
    col_blocks = local_cols // block_size
    col_kept = lax.dynamic_slice_in_dim(
        kept_blocks, lax.axis_index("cols") * col_blocks, col_blocks, 1
    )
    upper_masked = (
        upper_panels.reshape(subtree_count, upper_panels.shape[1], col_blocks, block_size)
        * col_kept[:, None, :, None]
    ).reshape(upper_panels.shape)
    upper_full = lax.all_gather(upper_masked, "rows", axis=1, tiled=True)
    applied_half = jnp.einsum(
        "sik,skc->sic", given_inverse, upper_full, preferred_element_type=jnp.float32
    ).astype(jnp.bfloat16)
    update = jnp.einsum(
        "sjqk,skc->jqc",
        lax.all_gather(lower_masked, "cols", axis=3, tiled=True),
        applied_half,
        preferred_element_type=jnp.float32,
    )
    negated = (-update).reshape(depth_count * rows_count, row_share, local_cols)
    owned_sum = lax.psum_scatter(negated, ("depth", "rows"), scatter_dimension=0, tiled=True)[0]
    ancestor = ancestor_entries + owned_sum
    first_row = lax.axis_index(("depth", "rows")) * row_share
    row_offset = jnp.arange(PW, dtype=jnp.int32) - first_row
    inside = (row_offset >= 0) & (row_offset < row_share)
    picked = jnp.take(ancestor, jnp.clip(row_offset, 0, row_share - 1), axis=0)
    picked = jnp.where(inside[:, None], picked, jnp.zeros_like(picked))
    top_block = lax.psum(picked, ("depth", "rows"))
    column_panel, pivot = (
        from_root(ancestor[:, :PW], "cols", 0),
        from_root(top_block[:, :PW], "cols", 0),
    )
    identity = jnp.eye(PW, dtype=jnp.float32)
    inverse = identity / 16.0
    for sweep in range(NEWTON):
        product = jnp.dot(pivot, inverse, precision=highest)
        inverse = jnp.dot(inverse, 2.0 * identity - product, precision=highest)
    column_factor = jnp.dot(column_panel, inverse, precision=highest)
    trailing = ancestor - jnp.dot(column_factor, top_block, precision=highest)
    return (column_factor, trailing)


def solution(mesh):
    return jax.shard_map(
        local,
        mesh=mesh,
        in_specs=(
            P("depth", None, None, ("rows", "cols")),
            P("depth", "rows", "cols"),
            P("depth", "rows", None),
            P("depth", None),
            P(("depth", "rows"), "cols"),
        ),
        out_specs=(P(("depth", "rows"), None), P(("depth", "rows"), "cols")),
        check_vma=False,
    )
```

profile of v0, /device:TPU:0, one launch (start us, length us, event | category | flops | bytes accessed | tf_op | source)
XLA Modules:
  0.0 562.5 jit_solution(16396072703336000724)
XLA Ops:
  7.2 0.0 copy-start
  7.2 0.0 all-gather.5.cloned.1.call-start
  7.2 0.8 compare_convert_fusion
  8.1 0.1 constant_dynamic-slice_fusion
  8.1 0.1 broadcast_bitcast_fusion
  8.2 2.7 broadcast_multiply_fusion
  10.9 0.0 all-gather.5.cloned.1.call-update
  10.9 0.0 all-gather.3.cloned.1.call-start
  11.0 0.1 mul.41
  11.0 0.1 mul.42
  11.1 2.7 copy_multiply_fusion
  13.8 0.0 all-gather.3.cloned.1.call-update
  13.8 0.0 reduce-scatter.2.cloned.1.call-start
  13.9 14.5 %all-gather.5.cloned.1.call-done = bf16[2,1024,768]{2,1,0:T(8,128)(2,1)} async-done(((bf16[2,512,768]{2,1,0:T(8,128)(2,1)}), bf16[2,1024,768]{2,1,0:T(8,128)(2,1)}) %all-gather.5.cloned.1.call-update) | async-done | bytes 3145744 | tf_op jit(solution)/shard_map/all_gather | solution.py:38
  28.3 151.1 %all-gather.3.cloned.1.call-done = bf16[2,8,768,512]{2,3,0,1:T(8,128)(2,1)} async-done(((bf16[2,8,768,64]{2,3,0,1:T(8,128)(2,1)}), bf16[2,8,768,512]{2,3,0,1:T(8,128)(2,1)}) %all-gather.3.cloned.1.call-update) | async-done | bytes 12582928 | tf_op jit(solution)/shard_map/all_gather | solution.py:44
  179.4 0.0 copy-done
  179.4 20.8 %bitcast_negate_fusion = f32[8,768,768]{2,1,0:T(8,128)} fusion(bf16[2,8,768,512]{2,3,0,1:T(8,128)(2,1)} %all-gather.3.cloned.1.call-done, bf16[2,512,1024]{2,1,0:T(8,128)(2,1)S(1)} %copy-done, bf16[2,1024,768]{2,1,0:T(8,128)(2,1)} %all-gather.5.cloned.1.call-done), kind=kOutput, calls=%fused_computation.1 | convolution fusion | flops 11279794176 | bytes 36700160 | tf_op jit(solution)/shard_map/sjqk,skc->jqc/dot_general | solution.py:42
  200.2 0.0 reduce-scatter.2.cloned.1.call-update
  200.2 0.0 all-reduce.4.cloned.1.call-start
  200.3 107.1 %reduce-scatter.2.cloned.1.call-done = f32[1,384,768]{2,1,0:T(8,128)} async-done(((f32[16,384,768]{2,1,0:T(8,128)}), f32[1,384,768]{2,1,0:T(8,128)}) %reduce-scatter.2.cloned.1.call-update) | async-done | bytes 1179664 | tf_op jit(solution)/shard_map/reduce_scatter | solution.py:49
  307.4 1.8 bitcast_add_fusion
  309.2 2.6 gather_fusion
  311.8 2.8 select_select_fusion
  314.6 0.0 all-reduce.4.cloned.1.call-update
  314.6 0.2 all-reduce.6.cloned.1.call-start
  314.8 1.0 slice_select_fusion.1
  315.8 119.0 %all-reduce.4.cloned.1.call-done = f32[512,768]{1,0:T(8,128)} async-done(((f32[512,768]{1,0:T(8,128)}), f32[512,768]{1,0:T(8,128)}) %all-reduce.4.cloned.1.call-update) | async-done | bytes 1572880 | tf_op jit(solution)/shard_map/psum | solution.py:56
  434.8 2.3 slice_select_fusion
  437.1 0.0 all-reduce.6.cloned.1.call-update
  437.1 105.7 %all-reduce.6.cloned.1.call-done = (f32[384,512]{1,0:T(8,128)}, f32[512,512]{1,0:T(8,128)}) async-done(((f32[384,512]{1,0:T(8,128)}, f32[512,512]{1,0:T(8,128)}), (f32[384,512]{1,0:T(8,128)}, f32[512,512]{1,0:T(8,128)})) %all-reduce.6.cloned.1.call-update) | async-done | bytes 1835024 | tf_op jit(solution)/shard_map/psum | solution.py:12
  542.8 3.0 select_subtract_fusion.1
  545.8 0.0 copy-start.3
  545.8 1.8 fusion.1
  547.6 0.0 copy-done.3
  547.7 1.9 select_subtract_fusion
  549.5 0.0 copy-start.4
  549.5 1.9 fusion.18
  551.4 0.0 copy-start.1
  551.4 0.0 copy-done.4
  551.4 1.4 fusion.19
  552.9 0.0 copy-done.1
  552.9 0.0 copy-start.2
  552.9 3.1 convolution_subtract_fusion
  556.0 0.0 copy-done.2
  (5 shorter events, 0.1 us)
Async XLA Ops:
  7.2 172.2 %copy-start = (bf16[2,512,1024]{2,1,0:T(8,128)(2,1)S(1)}, bf16[2,512,1024]{2,1,0:T(8,128)(2,1)}, u32[]{:S(2)}) copy-start(bf16[2,512,1024]{2,1,0:T(8,128)(2,1)} %param.7) | copy-start | bytes 6291460
  7.2 21.2 %all-gather.5.cloned.1.call-start = ((), (), s32[]{:S(2)}) async-start(), calls=%async_computation.2 | async-start | bytes 4718592 | tf_op jit(solution)/shard_map/all_gather | solution.py:38
  10.9 168.5 %all-gather.3.cloned.1.call-start = ((), (), s32[]{:S(2)}) async-start(), calls=%async_computation.1 | async-start | bytes 14155776 | tf_op jit(solution)/shard_map/all_gather | solution.py:44
  13.8 293.6 %reduce-scatter.2.cloned.1.call-start = ((), (), s32[]{:S(2)}) async-start(), calls=%async_computation.3 | async-start | bytes 20054016 | tf_op jit(solution)/shard_map/reduce_scatter | solution.py:49
  200.2 234.6 %all-reduce.4.cloned.1.call-start = ((), (), s32[]{:S(2)}) async-start(), calls=%async_computation.4 | async-start | bytes 3145728 | tf_op jit(solution)/shard_map/psum | solution.py:56
  314.6 228.2 %all-reduce.6.cloned.1.call-start = ((), (), s32[]{:S(2)}) async-start(), calls=%async_computation.5 | async-start | bytes 3670016 | tf_op jit(solution)/shard_map/psum | solution.py:12
  545.8 1.8 copy-start.3
  549.5 1.9 copy-start.4
  551.4 1.5 copy-start.1
  552.9 3.1 copy-start.2
Sparse Core Ops, SparseCore 0:
  11.0 17.2 all-gather.4
  30.7 148.6 all-gather.2
  200.3 107.0 reduce-scatter.1
  314.7 120.0 all-reduce.3
  438.0 104.7 all-reduce.5
where the time goes:
time: 563 us
  waiting for transfers between devices  497 us (88%)
  matrix products  33.9 us (6%)
  other arithmetic  14 us (2%)
  between operations  13.9 us (2%)
    all_gather x1, waiting for transfers between devices, local(): lax.all_gather(lower_masked, 'cols', axis=3, tiled=True)  151 us
    psum x1, waiting for transfers between devices, local(): top_block = lax.psum(picked, ('depth', 'rows'))  119 us
    reduce_scatter x1, waiting for transfers between devices, local(): lax.psum_scatter(negated, ('depth', 'rows'), scatter_dimension=0, tiled=T...  107 us
    psum x1, waiting for transfers between devices, from_root(): return lax.psum(jnp.where(mine, array, jnp.zeros_like(array)), axis)  106 us
    dot_general x1, matrix products, local(): jnp.einsum('sjqk,skc->jqc', lax.all_gather(lower_masked, 'cols', axis=3,...  20.8 us
    all_gather x1, waiting for transfers between devices, local(): upper_full = lax.all_gather(upper_masked, 'rows', axis=1, tiled=True)  14.5 us
  transfers between devices with their start and end apart: 5, of which 5 were waited for; matrix products, arithmetic and copies ran while one was open for 1% of the time, Pallas kernels for 0%

commit v1 on v0

--- a/solution.py
+++ b/solution.py
@@ -1,3 +1,4 @@
+import functools
 import jax
 import jax.numpy as jnp
 from jax import lax
@@ -5,6 +6,15 @@
 
 PW = 512
 NEWTON = 2
+
+
+def feed_ranges_here(point, dev_axis, d0):
+    z = jnp.stack([point for _ in range(lax.axis_size(dev_axis))])
+    outcome_arr = lax.all_to_all(z, dev_axis, 0, 0)
+    return jnp.concatenate(outcome_arr, d0)
+
+
+_touch_spots = functools.partial(feed_ranges_here, dev_axis="rows", d0=1)
 
 
 def from_root(array, axis, root):
@@ -35,7 +45,7 @@
         upper_panels.reshape(subtree_count, upper_panels.shape[1], col_blocks, block_size)
         * col_kept[:, None, :, None]
     ).reshape(upper_panels.shape)
-    upper_full = lax.all_gather(upper_masked, "rows", axis=1, tiled=True)
+    upper_full = _touch_spots(upper_masked)
     applied_half = jnp.einsum(
         "sik,skc->sic", given_inverse, upper_full, preferred_element_type=jnp.float32
     ).astype(jnp.bfloat16)

time: 563 us -> 543 us (0.964)
  waiting for transfers between devices: 497 us -> 472 us
  blocking collectives: 0 us -> 6.26 us
    all_gather x1 -> x0, waiting for transfers between devices: 14.5 us -> none  [local(): upper_full = lax.all_gather(upper_masked, 'rows', axis=1, tiled=True)]
    all_gather x1, waiting for transfers between devices: 151 us -> 140 us  [local(): lax.all_gather(lower_masked, 'cols', axis=3, tiled=True)]
    all_to_all x0 -> x1, blocking collectives: none -> 6.26 us  [feed_ranges_here(): outcome_arr = lax.all_to_all(z, dev_axis, 0, 0)]
  transfers between devices with their start and end apart: 5 -> 4, of which waited for: 5 -> 4; matrix products, arithmetic and copies ran while one was open for 1% -> 1% of each run, Pallas kernels for 0% -> 0%
where the time goes in v1:
time: 543 us
  waiting for transfers between devices  472 us (87%)
  matrix products  34.8 us (6%)
  between operations  14 us (3%)
  other arithmetic  11.4 us (2%)
  blocking collectives  6.26 us (1%)
    all_gather x1, waiting for transfers between devices, local(): lax.all_gather(lower_masked, 'cols', axis=3, tiled=True)  140 us
    psum x1, waiting for transfers between devices, local(): top_block = lax.psum(picked, ('depth', 'rows'))  119 us
    reduce_scatter x1, waiting for transfers between devices, local(): lax.psum_scatter(negated, ('depth', 'rows'), scatter_dimension=0, tiled=T...  107 us
    psum x1, waiting for transfers between devices, from_root(): return lax.psum(jnp.where(mine, array, jnp.zeros_like(array)), axis)  106 us
    dot_general x1, matrix products, local(): jnp.einsum('sjqk,skc->jqc', lax.all_gather(lower_masked, 'cols', axis=3,...  21.7 us
  transfers between devices with their start and end apart: 4, of which 4 were waited for; matrix products, arithmetic and copies ran while one was open for 1% of the time, Pallas kernels for 0%

profile of v1, /device:TPU:0, one launch (start us, length us, event | category | flops | bytes accessed | tf_op | source)
XLA Modules:
  0.0 542.7 jit_solution(9886980977338587647)
XLA Ops:
  7.2 0.0 copy-start
  7.2 0.0 all-gather.2.cloned.1.call-start
  7.2 0.8 compare_convert_fusion
  8.0 0.1 mul.44
  8.1 0.1 mul.45
  8.2 2.7 copy_multiply_fusion
  10.9 0.0 all-gather.2.cloned.1.call-update
  10.9 0.0 reduce-scatter.2.cloned.1.call-start
  11.0 0.1 constant_dynamic-slice_fusion
  11.1 0.1 broadcast_bitcast_fusion
  11.1 1.5 multiply_bitcast_fusion
  12.7 0.3 pad_maximum_fusion
  12.9 6.3 %all_to_all.5 = bf16[2,2,512,768]{3,2,1,0:T(8,128)(2,1)S(1)} all-to-all(bf16[2,2,512,768]{3,2,1,0:T(8,128)(2,1)S(1)} %pad_maximum_fusion), channel_id=1, replica_groups=mesh['depth'=8,'rows'=2,'cols'=8] {'rows'}, dimensions={0} | all-to-all | bytes 6291456 | tf_op jit(solution)/shard_map/all_to_all | solution.py:13
  19.2 1.8 copy.12
  21.0 139.8 %all-gather.2.cloned.1.call-done = bf16[2,8,768,512]{2,3,0,1:T(8,128)(2,1)} async-done(((bf16[2,8,768,64]{2,3,0,1:T(8,128)(2,1)}), bf16[2,8,768,512]{2,3,0,1:T(8,128)(2,1)}) %all-gather.2.cloned.1.call-update) | async-done | bytes 12582928 | tf_op jit(solution)/shard_map/all_gather | solution.py:54
  160.9 0.0 copy-done
  160.9 21.7 %bitcast_negate_fusion = f32[8,768,768]{2,1,0:T(8,128)} fusion(bf16[2,8,768,512]{2,3,0,1:T(8,128)(2,1)} %all-gather.2.cloned.1.call-done, bf16[2,1024,768]{2,1,0:T(8,128)(2,1)} %bitcast.44, bf16[2,512,1024]{2,1,0:T(8,128)(2,1)S(1)} %copy-done), kind=kOutput, calls=%fused_computation.1 | convolution fusion | flops 11279794176 | bytes 36700160 | tf_op jit(solution)/shard_map/sjqk,skc->jqc/dot_general | solution.py:52
  182.6 0.0 copy-start.4
  182.6 0.0 reduce-scatter.2.cloned.1.call-update
  182.6 0.0 all-reduce.4.cloned.1.call-start
  182.7 107.1 %reduce-scatter.2.cloned.1.call-done = f32[1,384,768]{2,1,0:T(8,128)} async-done(((f32[16,384,768]{2,1,0:T(8,128)}), f32[1,384,768]{2,1,0:T(8,128)}) %reduce-scatter.2.cloned.1.call-update) | async-done | bytes 1179664 | tf_op jit(solution)/shard_map/reduce_scatter | solution.py:59
  289.8 0.0 copy-done.4
  289.8 1.4 bitcast_add_fusion
  291.2 1.9 gather_fusion
  293.1 1.4 select_select_fusion
  294.5 0.0 all-reduce.4.cloned.1.call-update
  294.5 0.2 all-reduce.6.cloned.1.call-start
  294.7 1.0 slice_select_fusion.1
  295.7 119.0 %all-reduce.4.cloned.1.call-done = f32[512,768]{1,0:T(8,128)} async-done(((f32[512,768]{1,0:T(8,128)}), f32[512,768]{1,0:T(8,128)}) %all-reduce.4.cloned.1.call-update) | async-done | bytes 1572880 | tf_op jit(solution)/shard_map/psum | solution.py:66
  414.7 2.3 slice_select_fusion
  417.0 0.0 all-reduce.6.cloned.1.call-update
  417.0 105.9 %all-reduce.6.cloned.1.call-done = (f32[384,512]{1,0:T(8,128)}, f32[512,512]{1,0:T(8,128)}) async-done(((f32[384,512]{1,0:T(8,128)}, f32[512,512]{1,0:T(8,128)}), (f32[384,512]{1,0:T(8,128)}, f32[512,512]{1,0:T(8,128)})) %all-reduce.6.cloned.1.call-update) | async-done | bytes 1835024 | tf_op jit(solution)/shard_map/psum | solution.py:22
  522.9 3.0 select_subtract_fusion.1
  525.9 0.0 copy-start.5
  525.9 1.8 fusion.1
  527.7 0.0 copy-done.5
  527.8 1.9 select_subtract_fusion
  529.6 0.0 copy-start.6
  529.6 1.8 fusion.18
  531.5 0.0 copy-start.2
  531.5 0.0 copy-done.6
  531.5 0.0 copy-start.1
  531.5 1.4 fusion.19
  533.0 0.0 copy-done.2
  533.0 0.0 copy-start.3
  533.0 3.1 convolution_subtract_fusion
  536.1 0.0 copy-done.3
  536.1 0.0 copy-done.1
  (5 shorter events, 0.1 us)
Async XLA Ops:
  7.2 153.7 %copy-start = (bf16[2,512,1024]{2,1,0:T(8,128)(2,1)S(1)}, bf16[2,512,1024]{2,1,0:T(8,128)(2,1)}, u32[]{:S(2)}) copy-start(bf16[2,512,1024]{2,1,0:T(8,128)(2,1)} %param.7) | copy-start | bytes 6291460
  7.2 153.7 %all-gather.2.cloned.1.call-start = ((), (), s32[]{:S(2)}) async-start(), calls=%async_computation.2 | async-start | bytes 14155776 | tf_op jit(solution)/shard_map/all_gather | solution.py:54
  10.9 278.9 %reduce-scatter.2.cloned.1.call-start = ((), (), s32[]{:S(2)}) async-start(), calls=%async_computation.3 | async-start | bytes 20054016 | tf_op jit(solution)/shard_map/reduce_scatter | solution.py:59
  182.6 107.2 %copy-start.4 = (f32[384,768]{1,0:T(8,128)S(1)}, f32[384,768]{1,0:T(8,128)}, u32[]{:S(2)}) copy-start(f32[384,768]{1,0:T(8,128)} %param.9) | copy-start | bytes 3538948
  182.6 232.1 %all-reduce.4.cloned.1.call-start = ((), (), s32[]{:S(2)}) async-start(), calls=%async_computation.4 | async-start | bytes 3145728 | tf_op jit(solution)/shard_map/psum | solution.py:66
  294.5 228.4 %all-reduce.6.cloned.1.call-start = ((), (), s32[]{:S(2)}) async-start(), calls=%async_computation.5 | async-start | bytes 3670016 | tf_op jit(solution)/shard_map/psum | solution.py:22
  525.9 1.8 copy-start.5
  529.6 1.9 copy-start.6
  531.5 1.5 copy-start.2
  531.5 4.6 copy-start.1
  533.0 3.1 copy-start.3
Sparse Core Ops, SparseCore 0:
  11.0 149.7 all-gather.1
  182.7 107.0 reduce-scatter.1
  294.6 120.0 all-reduce.3
  417.9 104.9 all-reduce.5
